TPU v7x, 32 devices: a whole 2x2x4 slice. The times are simulated.
32 devices in a mesh: batch: 2 (over x), seq: 16 (over z, y, core).
Axes of the slice: x: 2, y: 2, z: 4, core: 2. Of those that a mesh axis runs over, the one named last changes fastest.
Arguments:
- tokens: bfloat16 [16, 2048, 640], P('batch', 'seq'), may hold values from -6 to 6
- attention_params: bfloat16 [1640192], P(('batch', 'seq')), may hold values from -1.3 to 1.3
- feed_params: bfloat16 [3933440], P(('batch', 'seq')), may hold values from -1.3 to 1.3
- positions: int32 [16, 2048], P('batch', 'seq'), may hold values from 0 to 2047, as said below
- cotangent: bfloat16 [16, 2048, 640], P('batch', 'seq'), may hold values from -6 to 6
Outputs:
- mixed: bfloat16 [16, 2048, 640], P('batch', 'seq')
- grad_tokens: float32 [16, 2048, 640], P('batch', 'seq')
- grad_attention: float32 [1640192], P(('batch', 'seq'))
- grad_feed: float32 [3933440], P(('batch', 'seq'))
Inputs may be any that keep to these rules, and one draw needn't show every extreme that they name: `positions`: in each sequence a position is one more than that of the token before it, or 0 where a document starts; every sequence starts a document at its first token and holds at most 4 documents; the first sequence is a single document.
All inputs are finite; a program needn't handle non-finite values.
Results may differ from a plain program's by a relative error of at most 0.012.
Values may be sent and summed in bfloat16 or wider, within the bound.
A program may use at most 192 MiB of HBM per device.

v0:
```python
import math

import jax
import jax.numpy as jnp
from jax import lax
from jax.sharding import PartitionSpec as P

D = 640
HEADS = 4
HEAD_DIM = 256
FF = 2048
WINDOW = 512


epsilon = 1e-06
rope_base = 10000.0


def shifted(block, axis, distance):
    devices = range(lax.axis_size(axis))
    route = [(i - distance, i) for i in devices if i - distance in devices]
    return lax.ppermute(block, axis, route)


def rms_norm(vector, scaling):
    return vector * lax.rsqrt(jnp.mean(vector * vector, axis=-1, keepdims=True) + epsilon) * scaling


def rotate(vector, cosine_table, sine_table):
    half_width = vector.shape[-1] // 2
    first_half = vector[..., :half_width]
    second_half = vector[..., half_width:]
    return jnp.concatenate(
        [
            first_half * cosine_table - second_half * sine_table,
            second_half * cosine_table + first_half * sine_table,
        ],
        axis=-1,
    )


def angles(positions):
    half_width = HEAD_DIM // 2
    frequency = rope_base ** (-(jnp.arange(half_width, dtype=jnp.float32) * 2.0 / HEAD_DIM))
    turned = positions.astype(jnp.float32)[..., None] * frequency
    return (jnp.cos(turned), jnp.sin(turned))


def split_flat(flat_vector, layouts):
    pieces = []
    offset = 0
    for layout in layouts:
        length = math.prod(layout)
        pieces.append(flat_vector[offset : offset + length].reshape(layout))
        offset += length
    return pieces


def attention_layouts():
    query_width = HEADS * HEAD_DIM
    return [
        (D, query_width),
        (D, HEAD_DIM),
        (D, HEAD_DIM),
        (query_width, D),
        (D,),
        (HEAD_DIM,),
        (HEAD_DIM,),
        (D,),
    ]


def feed_layouts():
    return [(D, FF), (D, FF), (FF, D), (D,), (D,)]


def contract_rows(left, right):
    return lax.dot_general(
        left, right, (((0,), (0,)), ((), ())), preferred_element_type=jnp.float32
    )


def contract_cols(left, right):
    return lax.dot_general(
        left, right, (((1,), (1,)), ((), ())), preferred_element_type=jnp.float32
    )


def flatten_all(arrays):
    return jnp.concatenate([array_item.reshape(-1) for array_item in arrays])


def on_device(tokens, attention_params, feed_params, positions, cotangent):
    seq_count, block, model_width = tokens.shape
    total_rows = seq_count * block
    halo_rows = WINDOW - 1
    hop_count = -(-halo_rows // block)
    needed_rows = [
        min(block, halo_rows - (hop_index - 1) * block) for hop_index in range(1, hop_count + 1)
    ]
    halo_starts = {}
    cursor = 0
    for hop_index in range(hop_count, 0, -1):
        halo_starts[hop_index] = cursor
        cursor += needed_rows[hop_index - 1]
    attention_flat, feed_flat = (
        lax.all_gather(attention_params, ("batch", "seq"), axis=0, tiled=True),
        lax.all_gather(feed_params, ("batch", "seq"), axis=0, tiled=True),
    )
    (
        weight_query,
        weight_key,
        weight_value,
        weight_out,
        gain_attention,
        gain_query,
        gain_key,
        gain_post,
    ) = split_flat(attention_flat, attention_layouts())
    gain_attention = gain_attention.astype(jnp.float32)
    gain_query = gain_query.astype(jnp.float32)
    gain_key = gain_key.astype(jnp.float32)
    gain_post = gain_post.astype(jnp.float32)
    inputs = tokens.astype(jnp.float32).reshape(total_rows, model_width)
    cosine_table, sine_table = angles(positions.reshape(total_rows))

    def query_prep(raw_rows, scaling):
        return rotate(rms_norm(raw_rows, scaling), cosine_table[:, None, :], sine_table[:, None, :])

    def key_prep(raw_rows, scaling):
        return rotate(rms_norm(raw_rows, scaling), cosine_table, sine_table)

    normed = rms_norm(inputs, gain_attention).astype(jnp.bfloat16)
    query_raw = jnp.dot(normed, weight_query, preferred_element_type=jnp.float32).reshape(
        total_rows, HEADS, HEAD_DIM
    )
    key_raw = jnp.dot(normed, weight_key, preferred_element_type=jnp.float32)
    value_raw = jnp.dot(normed, weight_value, preferred_element_type=jnp.float32)
    queries = (
        query_prep(query_raw, gain_query)
        .astype(jnp.bfloat16)
        .reshape(seq_count, block, HEADS, HEAD_DIM)
    )
    key_rows = key_prep(key_raw, gain_key).astype(jnp.bfloat16).reshape(seq_count, block, HEAD_DIM)
    value_rows = value_raw.astype(jnp.bfloat16).reshape(seq_count, block, HEAD_DIM)
    halo_keys = []
    halo_values = []
    for hop_index in range(1, hop_count + 1):
        needed = needed_rows[hop_index - 1]
        got_keys, got_values = shifted(
            (key_rows[:, block - needed :], value_rows[:, block - needed :]), "seq", hop_index
        )
        halo_keys.insert(0, got_keys)
        halo_values.insert(0, got_values)
    extended_keys = jnp.concatenate(halo_keys + [key_rows], axis=1)
    extended_values = jnp.concatenate(halo_values + [value_rows], axis=1)
    extended_len = halo_rows + block
    distance = (
        jnp.arange(block, dtype=jnp.int32)[:, None]
        + halo_rows
        - jnp.arange(extended_len, dtype=jnp.int32)[None, :]
    )
    allowed = (distance >= 0) & (distance < WINDOW)
    allowed = allowed[None] & (distance[None] <= positions[:, :, None])
    allowed = allowed[:, None]
    score_scale = HEAD_DIM ** (-0.5)

    def score_of(query_block, key_block):
        logits = jnp.einsum(
            "sqhd,skd->shqk", query_block, key_block, preferred_element_type=jnp.float32
        )
        return jnp.where(allowed, logits * score_scale, -1e30)

    scores = score_of(queries, extended_keys)
    row_peak = jnp.max(scores, axis=-1, keepdims=True)
    raised = jnp.exp(scores - row_peak)
    row_total = jnp.sum(raised, axis=-1, keepdims=True)
    probability = raised / row_total
    log_total = row_peak + jnp.log(row_total)
    weights_rounded = probability.astype(jnp.bfloat16)
    attended = jnp.einsum(
        "shqk,skd->sqhd", weights_rounded, extended_values, preferred_element_type=jnp.float32
    )
    merged = attended.reshape(total_rows, HEADS * HEAD_DIM).astype(jnp.bfloat16)
    projected = jnp.dot(merged, weight_out, preferred_element_type=jnp.float32)
    hidden_state = inputs + rms_norm(projected, gain_post)
    weight_gate, weight_up, weight_down, gain_feed, gain_out = split_flat(feed_flat, feed_layouts())
    gain_feed = gain_feed.astype(jnp.float32)
    gain_out = gain_out.astype(jnp.float32)

    def gated(gate_values, up_values):
        return jax.nn.gelu(gate_values, approximate=True) * up_values

    feed_in = rms_norm(hidden_state, gain_feed).astype(jnp.bfloat16)
    gate_values = jnp.dot(feed_in, weight_gate, preferred_element_type=jnp.float32)
    up_values = jnp.dot(feed_in, weight_up, preferred_element_type=jnp.float32)
    activation = gated(gate_values, up_values).astype(jnp.bfloat16)
    down_values = jnp.dot(activation, weight_down, preferred_element_type=jnp.float32)
    output = hidden_state + rms_norm(down_values, gain_out)
    mixed = output.astype(jnp.bfloat16).reshape(seq_count, block, model_width)
    grad_output = cotangent.astype(jnp.float32).reshape(total_rows, model_width)
    unused, pullback = jax.vjp(rms_norm, down_values, gain_out)
    grad_down, grad_gain_out = pullback(grad_output)
    grad_down = grad_down.astype(jnp.bfloat16)
    grad_weight_down = contract_rows(activation, grad_down)
    grad_activation = contract_cols(grad_down, weight_down)
    unused, pullback = jax.vjp(gated, gate_values, up_values)
    grad_gate, grad_up = pullback(grad_activation)
    grad_gate = grad_gate.astype(jnp.bfloat16)
    grad_up = grad_up.astype(jnp.bfloat16)
    grad_weight_gate = contract_rows(feed_in, grad_gate)
    grad_weight_up = contract_rows(feed_in, grad_up)
    grad_feed_in = contract_cols(grad_gate, weight_gate) + contract_cols(grad_up, weight_up)
    unused, pullback = jax.vjp(rms_norm, hidden_state, gain_feed)
    grad_hidden_part, grad_gain_feed = pullback(grad_feed_in)
    grad_hidden = grad_output + grad_hidden_part
    feed_grads = flatten_all(
        [grad_weight_gate, grad_weight_up, grad_weight_down, grad_gain_feed, grad_gain_out]
    )
    unused, pullback = jax.vjp(rms_norm, projected, gain_post)
    grad_projected, grad_gain_post = pullback(grad_hidden)
    grad_projected = grad_projected.astype(jnp.bfloat16)
    grad_weight_out = contract_rows(merged, grad_projected)
    grad_merged = (
        contract_cols(grad_projected, weight_out)
        .astype(jnp.bfloat16)
        .reshape(seq_count, block, HEADS, HEAD_DIM)
    )
    scores = score_of(queries, extended_keys)
    probability = jnp.exp(scores - log_total)
    weights_rounded = probability.astype(jnp.bfloat16)
    grad_probs = jnp.einsum(
        "sqhd,skd->shqk", grad_merged, extended_values, preferred_element_type=jnp.float32
    )
    inner = jnp.sum(probability * grad_probs, axis=-1, keepdims=True)
    grad_logits = (probability * (grad_probs - inner) * score_scale).astype(jnp.bfloat16)
    grad_queries = jnp.einsum(
        "shqk,skd->sqhd", grad_logits, extended_keys, preferred_element_type=jnp.float32
    )
    grad_ext_keys = jnp.einsum(
        "shqk,sqhd->skd", grad_logits, queries, preferred_element_type=jnp.float32
    )
    grad_ext_values = jnp.einsum(
        "shqk,sqhd->skd", weights_rounded, grad_merged, preferred_element_type=jnp.float32
    )

    def halo_part(array_item, hop_index):
        first_row = halo_starts[hop_index]
        return array_item[:, first_row : first_row + needed_rows[hop_index - 1]]

    local_keys_grad = grad_ext_keys[:, halo_rows:]
    local_values_grad = grad_ext_values[:, halo_rows:]
    for hop_index in range(1, hop_count + 1):
        needed = needed_rows[hop_index - 1]
        back_keys, back_values = (
            shifted(
                halo_part(grad_ext_keys, hop_index).astype(jnp.bfloat16), "seq", -hop_index
            ).astype(jnp.float32),
            shifted(
                halo_part(grad_ext_values, hop_index).astype(jnp.bfloat16), "seq", -hop_index
            ).astype(jnp.float32),
        )
        local_keys_grad = local_keys_grad.at[:, block - needed :].add(back_keys)
        local_values_grad = local_values_grad.at[:, block - needed :].add(back_values)
    unused, pullback = jax.vjp(query_prep, query_raw, gain_query)
    grad_query_raw, grad_gain_query = pullback(grad_queries.reshape(total_rows, HEADS, HEAD_DIM))
    grad_query_raw = grad_query_raw.reshape(total_rows, HEADS * HEAD_DIM).astype(jnp.bfloat16)
    unused, pullback = jax.vjp(key_prep, key_raw, gain_key)
    grad_key_raw, grad_gain_key = pullback(local_keys_grad.reshape(total_rows, HEAD_DIM))
    grad_key_raw = grad_key_raw.astype(jnp.bfloat16)
    grad_value_raw = local_values_grad.reshape(total_rows, HEAD_DIM).astype(jnp.bfloat16)
    grad_weight_query = contract_rows(normed, grad_query_raw)
    grad_weight_key = contract_rows(normed, grad_key_raw)
    grad_weight_value = contract_rows(normed, grad_value_raw)
    grad_normed = (
        contract_cols(grad_query_raw, weight_query)
        + contract_cols(grad_key_raw, weight_key)
        + contract_cols(grad_value_raw, weight_value)
    )
    unused, pullback = jax.vjp(rms_norm, inputs, gain_attention)
    grad_input_part, grad_gain_attention = pullback(grad_normed)
    grad_tokens = (grad_hidden + grad_input_part).reshape(seq_count, block, model_width)
    attention_grads = flatten_all(
        [
            grad_weight_query,
            grad_weight_key,
            grad_weight_value,
            grad_weight_out,
            grad_gain_attention,
            grad_gain_query,
            grad_gain_key,
            grad_gain_post,
        ]
    )
    attention_piece, feed_piece = (
        lax.psum_scatter(attention_grads, ("batch", "seq"), scatter_dimension=0, tiled=True),
        lax.psum_scatter(feed_grads, ("batch", "seq"), scatter_dimension=0, tiled=True),
    )
    return (mixed, grad_tokens, attention_piece, feed_piece)


def solution(mesh):
    return jax.shard_map(
        on_device,
        mesh=mesh,
        in_specs=(
            P("batch", "seq", None),
            P(("batch", "seq")),
            P(("batch", "seq")),
            P("batch", "seq"),
            P("batch", "seq", None),
        ),
        out_specs=(
            P("batch", "seq", None),
            P("batch", "seq", None),
            P(("batch", "seq")),
            P(("batch", "seq")),
        ),
        check_vma=False,
    )
```

profile of v0, /device:TPU:0, one launch (start us, length us, event | category | flops | bytes accessed | tf_op | source)
XLA Modules:
  0.0 999.7 jit_solution(14183992160428053491)
XLA Ops:
  9.2 3.5 broadcast.557
  13.3 4.7 dynamic-update-slice.19
  21.1 218.2 %all-reduce.15.cloned.1.call-done = (bf16[1640192]{0:T(1024)(128)(2,1)}, bf16[3933440]{0:T(1024)(128)(2,1)}) async-done(((bf16[1640192]{0:T(1024)(128)(2,1)}, bf16[3933440]{0:T(1024)(128)(2,1)}), (bf16[1640192]{0:T(1024)(128)(2,1)}, bf16[3933440]{0:T(1024)(128)(2,1)})) %all-reduce.15.cloned.1.call-update) | async-done | bytes 11147280
  240.9 6.0 fusion.93
  251.9 3.1 multiply_cosine_fusion
  258.9 3.5 collective-permute-start.6
  262.4 3.9 collective-permute-start.5
  266.3 3.3 reshape.645
  272.1 2.9 collective-permute-start.4
  277.4 3.7 multiply_reduce_fusion.2
  291.9 5.5 slice.307
  299.2 5.2 reshape.648
  304.4 5.3 reshape.647
  309.7 4.1 subtract_convert_fusion
  313.8 3.5 collective-permute-start.2
  322.6 20.2 %concatenate.50 = bf16[8,639,256]{2,1,0:T(8,128)(2,1)} concatenate(bf16[8,127,256]{2,1,0:T(8,128)(2,1)} %collective-permute-done.4, bf16[8,128,256]{2,1,0:T(8,128)(2,1)} %collective-permute-done.5, bf16[8,128,256]{2,1,0:T(8,128)(2,1)} %collective-permute-done.6, bf16[8,128,256]{2,1,0:T(8,128)(2,1)} %collective-permute-done.7, bf16[8,128,256]{2,1,0:T(8,128)(2,1)} %pad_maximum_fusion.1), dimensions={1} | concatenate | bytes 5234688 | tf_op jit(solution)/shard_map/concatenate | solution.py:155
  342.8 3.8 fusion.98
  350.6 5.6 concatenate.46
  356.3 6.7 convert_bitcast_fusion
  368.9 3.4 fusion.101
  372.3 7.7 multiply_convert_fusion.1
  380.1 5.7 multiply_reduce_fusion.7
  389.0 13.6 %multiply_convert_fusion = (bf16[1024,2048]{1,0:T(8,128)(2,1)}, bf16[1024,2048]{1,0:T(8,128)(2,1)}) fusion(f32[1024,2048]{1,0:T(8,128)} %copy-done.66, f32[1024,2048]{1,0:T(8,128)} %get-tuple-element.211, bf16[1024,640]{1,0:T(8,128)(2,1)S(1)} %get-tuple-element.186, bf16[2048,640]{1,0:T(8,128)(2,1)S(1)} %copy-done.25), kind=kOutput, calls=%fused_computation.20 | convolution fusion | flops 2734686208 | bytes 29097984 | tf_op jit(solution)/shard_map/dot_general | solution.py:84
  402.6 5.5 fusion.102
  408.1 4.0 multiply_reduce_fusion.3
  415.7 3.3 fusion.48
  419.1 3.2 convolution_convert_fusion
  422.2 4.8 convolution_bitcast_fusion
  427.0 4.8 convolution_bitcast_fusion.1
  431.8 5.2 fusion.105
  437.0 3.3 reshape.652
  440.3 6.6 fusion.28
  447.0 18.5 %fusion.45 = f32[8,128,4,256]{3,1,2,0:T(8,128)} fusion(f32[8,639,128,4]{2,1,3,0:T(8,128)} %fusion.28, f32[8,4,128,639]{2,3,1,0:T(8,128)} %copy-done.2, f32[8,4,128]{2,1,0:T(4,128)S(1)} %bitcast.228, bf16[8,639,256]{2,1,0:T(8,128)(2,1)} %concatenate.50), kind=kOutput, calls=%fused_computation.85 | convolution fusion | flops 1358406272 | bytes 27766784 | tf_op jit(solution)/shard_map/shqk,skd->sqhd/dot_general | solution.py:237
  465.5 19.7 %fusion.99 = (bf16[8,639,256]{2,1,0:T(8,128)(2,1)}, f32[8,639,256]{2,1,0:T(8,128)}) fusion(f32[8,639,128,4]{2,1,3,0:T(8,128)} %fusion.28, f32[8,4,128,639]{2,3,1,0:T(8,128)} %copy-done.2, f32[8,4,128]{2,1,0:T(4,128)S(1)} %bitcast.229, bf16[8,128,4,128]{3,1,0,2:T(8,128)(2,1)} %bitcast.224, bf16[8,128,4,128]{3,1,0,2:T(8,128)(2,1)S(1)} %bitcast.222), kind=kOutput, calls=%fused_computation.200 | convolution fusion | flops 1363909248 | bytes 30904320 | tf_op jit(solution)/shard_map/shqk,sqhd->skd/dot_general | solution.py:240
  485.1 8.9 fusion.100
  498.7 3.7 reshape.659
  502.4 6.2 copy.72
  508.6 3.5 copy.73
  512.2 6.5 reshape.662
  535.5 3.3 convolution_bitcast_fusion.2
  541.1 2.9 constant_dynamic-update-slice_fusion.1
  543.9 2.9 constant_dynamic-update-slice_fusion.12
  547.8 2.8 constant_dynamic-update-slice_fusion.11
  551.7 3.3 fusion.103
  564.8 21.6 %collective-permute-done.11 = bf16[8,127,256]{2,1,0:T(8,128)(2,1)S(1)} collective-permute-done((bf16[8,127,256]{2,1,0:T(8,128)(2,1)}, bf16[8,127,256]{2,1,0:T(8,128)(2,1)S(1)}, u32[]{:S(2)}, u32[]{:S(2)}) %collective-permute-start.11) | collective-permute-done | bytes 520224 | tf_op jit(solution)/shard_map/ppermute | solution.py:22
  598.0 15.6 %collective-permute-done.15 = bf16[8,127,256]{2,1,0:T(8,128)(2,1)} collective-permute-done((bf16[8,127,256]{2,1,0:T(8,128)(2,1)}, bf16[8,127,256]{2,1,0:T(8,128)(2,1)}, u32[]{:S(2)}, u32[]{:S(2)}) %collective-permute-start.15) | collective-permute-done | bytes 520224 | tf_op jit(solution)/shard_map/ppermute | solution.py:22
  633.5 4.7 fusion.26
  638.1 350.8 %all-reduce.13.cloned.1.call-done = (f32[1640192]{0:T(1024)}, f32[3933440]{0:T(1024)}) async-done(((f32[1640192]{0:T(1024)}, f32[3933440]{0:T(1024)}), (f32[1640192]{0:T(1024)}, f32[3933440]{0:T(1024)})) %all-reduce.13.cloned.1.call-update) | async-done | bytes 22294544
  (274 shorter events, 126.0 us)
Async XLA Ops:
  7.2 232.2 %all-reduce.15.cloned.1.call-start = ((), (), s32[]{:S(2)}) async-start(), calls=%async_computation.1 | async-start | bytes 22298624
  18.0 970.9 %all-reduce.13.cloned.1.call-start = ((), (), s32[]{:S(2)}) async-start(), calls=%async_computation | async-start | bytes 44597248
  19.3 232.5 %copy-start.62 = (f32[128]{0:T(128)}, f32[128]{0:T(128)S(1)}, u32[]{:S(2)}) copy-start(f32[128]{0:T(128)S(1)} %negate_power_fusion) | copy-start | bytes 1540
  19.6 227.3 %copy-start.49 = (f32[8,128]{1,0:T(8,128)}, f32[8,128]{1,0:T(8,128)S(1)}, u32[]{:S(2)}) copy-start(f32[8,128]{1,0:T(8,128)S(1)} %fusion.37) | copy-start | bytes 12292
  19.7 229.9 %copy-start.45 = (f32[1024]{0:T(1024)}, f32[1024]{0:T(1024)S(1)}, u32[]{:S(2)}) copy-start(f32[1024]{0:T(1024)S(1)} %bitcast_rsqrt_fusion) | copy-start | bytes 12292
  19.7 232.1 %copy-start.53 = (f32[1024]{0:T(1024)}, f32[1024]{0:T(1024)S(1)}, u32[]{:S(2)}) copy-start(f32[1024]{0:T(1024)S(1)} %convert_bitcast_fusion.1) | copy-start | bytes 12292
  240.1 10.6 %copy-start.57 = (f32[256]{0:T(256)}, f32[256]{0:T(256)S(1)}, u32[]{:S(2)}) copy-start(f32[256]{0:T(256)S(1)} %get-tuple-element.181) | copy-start | bytes 3076
  240.1 41.0 %copy-start.60 = (f32[256]{0:T(256)}, f32[256]{0:T(256)S(1)}, u32[]{:S(2)}) copy-start(f32[256]{0:T(256)S(1)} %get-tuple-element.180) | copy-start | bytes 3076
  240.9 29.8 %copy-start.43 = (f32[640]{0:T(1024)}, f32[640]{0:T(1024)S(1)}, u32[]{:S(2)}) copy-start(f32[640]{0:T(1024)S(1)} %get-tuple-element.221) | copy-start | bytes 7684
  240.9 6.6 copy-start.21
  250.6 5.2 copy-start.6
  250.6 18.9 %copy-start.55 = (f32[1024]{0:T(1024)}, f32[1024]{0:T(1024)S(1)}, u32[]{:S(2)}) copy-start(f32[1024]{0:T(1024)S(1)} %get-tuple-element.202) | copy-start | bytes 12292
  254.9 54.8 %copy-start.16 = (f32[1024,128]{1,0:T(8,128)}, f32[1024,128]{1,0:T(8,128)S(1)}, u32[]{:S(2)}) copy-start(f32[1024,128]{1,0:T(8,128)S(1)} %get-tuple-element.198) | copy-start | bytes 1572868
  256.8 60.5 %collective-permute-start.7 = (bf16[8,128,256]{2,1,0:T(8,128)(2,1)}, bf16[8,128,256]{2,1,0:T(8,128)(2,1)}, u32[]{:S(2)}, u32[]{:S(2)}) collective-permute-start(bf16[8,128,256]{2,1,0:T(8,128)(2,1)} %pad_maximum_fusion.1), channel_id=1, source_target_pairs={{0,1},{1,2},{2,3},{3,4},{4,5},{5,6},{6,7},{7,8},{8,9},{9,10},{10,1... | collective-permute-start | bytes 1572872 | tf_op jit(solution)/shard_map/ppermute | solution.py:22
  258.9 61.2 %collective-permute-start.6 = (bf16[8,128,256]{2,1,0:T(8,128)(2,1)}, bf16[8,128,256]{2,1,0:T(8,128)(2,1)}, u32[]{:S(2)}, u32[]{:S(2)}) collective-permute-start(bf16[8,128,256]{2,1,0:T(8,128)(2,1)} %pad_maximum_fusion.1), channel_id=1, source_target_pairs={{0,2},{1,3},{2,4},{3,5},{4,6},{5,7},{6,8},{7,9},{8,10},{9,11},{10,... | collective-permute-start | bytes 1572872 | tf_op jit(solution)/shard_map/ppermute | solution.py:22
  262.4 60.2 %collective-permute-start.5 = (bf16[8,128,256]{2,1,0:T(8,128)(2,1)}, bf16[8,128,256]{2,1,0:T(8,128)(2,1)}, u32[]{:S(2)}, u32[]{:S(2)}) collective-permute-start(bf16[8,128,256]{2,1,0:T(8,128)(2,1)} %pad_maximum_fusion.1), channel_id=1, source_target_pairs={{0,3},{1,4},{2,5},{3,6},{4,7},{5,8},{6,9},{7,10},{8,11},{9,12},{10... | collective-permute-start | bytes 1572872 | tf_op jit(solution)/shard_map/ppermute | solution.py:22
  270.7 12.8 %copy-start.30 = (bf16[640,256]{1,0:T(8,128)(2,1)}, bf16[640,256]{1,0:T(8,128)(2,1)S(1)}, u32[]{:S(2)}) copy-start(bf16[640,256]{1,0:T(8,128)(2,1)S(1)} %slice.289) | copy-start | bytes 983044
  272.1 41.7 %collective-permute-start.4 = (bf16[8,127,256]{2,1,0:T(8,128)(2,1)}, bf16[8,127,256]{2,1,0:T(8,128)(2,1)}, u32[]{:S(2)}, u32[]{:S(2)}) collective-permute-start(bf16[8,127,256]{2,1,0:T(8,128)(2,1)} %fusion.73), channel_id=1, source_target_pairs={{0,4},{1,5},{2,6},{3,7},{4,8},{5,9},{6,10},{7,11},{8,12},{9,13},{1... | collective-permute-start | bytes 1560584 | tf_op jit(solution)/shard_map/ppermute | solution.py:22
  289.8 60.8 %collective-permute-start.3 = (bf16[8,128,256]{1,2,0:T(8,128)(2,1)}, bf16[8,128,256]{1,2,0:T(8,128)(2,1)}, u32[]{:S(2)}, u32[]{:S(2)}) collective-permute-start(bf16[8,128,256]{1,2,0:T(8,128)(2,1)} %copy.40), channel_id=1, source_target_pairs={{0,1},{1,2},{2,3},{3,4},{4,5},{5,6},{6,7},{7,8},{8,9},{9,10},{10,1... | collective-permute-start | bytes 1572872 | tf_op jit(solution)/shard_map/ppermute | solution.py:22
  304.4 5.3 copy-start.18
  313.8 29.0 %copy-start.37 = (bf16[1024,4,128]{2,0,1:T(8,128)(2,1)S(1)}, bf16[1024,4,128]{2,0,1:T(8,128)(2,1)}, u32[]{:S(2)}) copy-start(bf16[1024,4,128]{2,0,1:T(8,128)(2,1)} %get-tuple-element.176) | copy-start | bytes 3145732
  313.8 36.8 %collective-permute-start.2 = (bf16[8,128,256]{1,2,0:T(8,128)(2,1)S(1)}, bf16[8,128,256]{1,2,0:T(8,128)(2,1)S(1)}, u32[]{:S(2)}, u32[]{:S(2)}) collective-permute-start(bf16[8,128,256]{1,2,0:T(8,128)(2,1)S(1)} %copy-done.20), channel_id=1, source_target_pairs={{0,2},{1,3},{2,4},{3,5},{4,6},{5,7},{6,8},{7,9},{8,10},{9,11},{10,... | collective-permute-start | bytes 1572872 | tf_op jit(solution)/shard_map/ppermute | solution.py:22
  317.3 33.3 %collective-permute-start.1 = (bf16[8,128,256]{1,2,0:T(8,128)(2,1)S(1)}, bf16[8,128,256]{1,2,0:T(8,128)(2,1)}, u32[]{:S(2)}, u32[]{:S(2)}) collective-permute-start(bf16[8,128,256]{1,2,0:T(8,128)(2,1)S(1)} %copy-done.20), channel_id=1, source_target_pairs={{0,3},{1,4},{2,5},{3,6},{4,7},{5,8},{6,9},{7,10},{8,11},{9,12},{10... | collective-permute-start | bytes 1572872 | tf_op jit(solution)/shard_map/ppermute | solution.py:22
  320.1 30.5 %collective-permute-start = (bf16[8,127,256]{1,2,0:T(8,128)(2,1)}, bf16[8,127,256]{1,2,0:T(8,128)(2,1)}, u32[]{:S(2)}, u32[]{:S(2)}) collective-permute-start(bf16[8,127,256]{1,2,0:T(8,128)(2,1)} %slice.323), channel_id=1, source_target_pairs={{0,4},{1,5},{2,6},{3,7},{4,8},{5,9},{6,10},{7,11},{8,12},{9,13},{1... | collective-permute-start | bytes 1560584 | tf_op jit(solution)/shard_map/ppermute | solution.py:22
  372.3 7.7 copy-start.66
  372.3 7.7 copy-start.25
  380.1 5.7 copy-start.9
  402.6 5.5 copy-start.65
  447.0 18.5 %copy-start.38 = (bf16[1024,4,128]{2,0,1:T(8,128)(2,1)S(1)}, bf16[1024,4,128]{2,0,1:T(8,128)(2,1)}, u32[]{:S(2)}) copy-start(bf16[1024,4,128]{2,0,1:T(8,128)(2,1)} %get-tuple-element.176) | copy-start | bytes 3145732
  485.1 8.9 copy-start.29
  498.7 9.9 slice-start.6
  502.4 6.3 slice-start.7
  526.4 9.1 copy-start.32
  528.8 67.2 %collective-permute-start.12 = (bf16[8,128,256]{2,1,0:T(8,128)(2,1)}, bf16[8,128,256]{2,1,0:T(8,128)(2,1)}, u32[]{:S(2)}, u32[]{:S(2)}) collective-permute-start(bf16[8,128,256]{2,1,0:T(8,128)(2,1)} %get-tuple-element.188), channel_id=1, source_target_pairs={{1,0},{2,1},{3,2},{4,3},{5,4},{6,5},{7,6},{8,7},{9,8},{10,9},{11,1... | collective-permute-start | bytes 1572872 | tf_op jit(solution)/shard_map/ppermute | solution.py:22
  530.1 27.6 %collective-permute-start.8 = (bf16[8,128,256]{2,1,0:T(8,128)(2,1)}, bf16[8,128,256]{2,1,0:T(8,128)(2,1)S(1)}, u32[]{:S(2)}, u32[]{:S(2)}) collective-permute-start(bf16[8,128,256]{2,1,0:T(8,128)(2,1)} %get-tuple-element.191), channel_id=1, source_target_pairs={{1,0},{2,1},{3,2},{4,3},{5,4},{6,5},{7,6},{8,7},{9,8},{10,9},{11,1... | collective-permute-start | bytes 1572872 | tf_op jit(solution)/shard_map/ppermute | solution.py:22
  531.4 27.6 %collective-permute-start.10 = (bf16[8,128,256]{2,1,0:T(8,128)(2,1)}, bf16[8,128,256]{2,1,0:T(8,128)(2,1)S(1)}, u32[]{:S(2)}, u32[]{:S(2)}) collective-permute-start(bf16[8,128,256]{2,1,0:T(8,128)(2,1)} %get-tuple-element.192), channel_id=1, source_target_pairs={{3,0},{4,1},{5,2},{6,3},{7,4},{8,5},{9,6},{10,7},{11,8},{12,9},{13... | collective-permute-start | bytes 1572872 | tf_op jit(solution)/shard_map/ppermute | solution.py:22
  532.7 29.2 %collective-permute-start.9 = (bf16[8,128,256]{2,1,0:T(8,128)(2,1)}, bf16[8,128,256]{2,1,0:T(8,128)(2,1)S(1)}, u32[]{:S(2)}, u32[]{:S(2)}) collective-permute-start(bf16[8,128,256]{2,1,0:T(8,128)(2,1)} %get-tuple-element.193), channel_id=1, source_target_pairs={{2,0},{3,1},{4,2},{5,3},{6,4},{7,5},{8,6},{9,7},{10,8},{11,9},{12,... | collective-permute-start | bytes 1572872 | tf_op jit(solution)/shard_map/ppermute | solution.py:22
  534.0 52.4 %collective-permute-start.11 = (bf16[8,127,256]{2,1,0:T(8,128)(2,1)}, bf16[8,127,256]{2,1,0:T(8,128)(2,1)S(1)}, u32[]{:S(2)}, u32[]{:S(2)}) collective-permute-start(bf16[8,127,256]{2,1,0:T(8,128)(2,1)} %slice.346), channel_id=1, source_target_pairs={{4,0},{5,1},{6,2},{7,3},{8,4},{9,5},{10,6},{11,7},{12,8},{13,9},{1... | collective-permute-start | bytes 1560584 | tf_op jit(solution)/shard_map/ppermute | solution.py:22
  535.5 5.6 slice-start.2
  538.8 5.1 slice-start.4
  541.1 6.2 slice-start
  557.7 38.3 %collective-permute-start.14 = (bf16[8,128,256]{2,1,0:T(8,128)(2,1)}, bf16[8,128,256]{2,1,0:T(8,128)(2,1)}, u32[]{:S(2)}, u32[]{:S(2)}) collective-permute-start(bf16[8,128,256]{2,1,0:T(8,128)(2,1)} %get-tuple-element.189), channel_id=1, source_target_pairs={{3,0},{4,1},{5,2},{6,3},{7,4},{8,5},{9,6},{10,7},{11,8},{12,9},{13... | collective-permute-start | bytes 1572872 | tf_op jit(solution)/shard_map/ppermute | solution.py:22
  559.0 37.0 %collective-permute-start.13 = (bf16[8,128,256]{2,1,0:T(8,128)(2,1)}, bf16[8,128,256]{2,1,0:T(8,128)(2,1)}, u32[]{:S(2)}, u32[]{:S(2)}) collective-permute-start(bf16[8,128,256]{2,1,0:T(8,128)(2,1)} %get-tuple-element.190), channel_id=1, source_target_pairs={{2,0},{3,1},{4,2},{5,3},{6,4},{7,5},{8,6},{9,7},{10,8},{11,9},{12,... | collective-permute-start | bytes 1572872 | tf_op jit(solution)/shard_map/ppermute | solution.py:22
  561.9 51.6 %collective-permute-start.15 = (bf16[8,127,256]{2,1,0:T(8,128)(2,1)}, bf16[8,127,256]{2,1,0:T(8,128)(2,1)}, u32[]{:S(2)}, u32[]{:S(2)}) collective-permute-start(bf16[8,127,256]{2,1,0:T(8,128)(2,1)} %slice.352), channel_id=1, source_target_pairs={{4,0},{5,1},{6,2},{7,3},{8,4},{9,5},{10,6},{11,7},{12,8},{13,9},{1... | collective-permute-start | bytes 1560584 | tf_op jit(solution)/shard_map/ppermute | solution.py:22
  564.8 24.5 %copy-start.54 = (f32[1024]{0:T(1024)S(1)}, f32[1024]{0:T(1024)}, u32[]{:S(2)}) copy-start(f32[1024]{0:T(1024)} %copy-done.53) | copy-start | bytes 12292
  564.8 24.5 %copy-start.63 = (f32[128]{0:T(128)S(1)}, f32[128]{0:T(128)}, u32[]{:S(2)}) copy-start(f32[128]{0:T(128)} %copy-done.62) | copy-start | bytes 1540
  586.6 5.0 copy-start.7
  586.6 5.0 copy-start.48
  (46 other events, 133.1 us)
Sparse Core Ops, SparseCore 0:
  18.1 221.1 all-reduce.14
  632.9 355.9 all-reduce.12
where the time goes:
time: 1020 us; the launch traced here: 1000 us
  waiting for transfers between devices  608 us (60%)
  local copies, waits for them, and re-layouts  155 us (15%)
  matrix products  146 us (14%)
  other arithmetic  41.9 us (4%)
  starting transfers between devices  33.7 us (3%)
  between operations  15.3 us (2%)
    unnamed x4, waiting for transfers between devices  569 us
    unnamed x174, local copies, waits for them, and re-layouts  59.8 us
    ppermute x16, waiting for transfers between devices, shifted(): return lax.ppermute(block, axis, route)  38.9 us
    dot_general x7, matrix products, contract_cols(): lax.dot_general(left, right, (((1,), (1,)), ((), ())), preferred_element_...  34.3 us
    ppermute x16, starting transfers between devices, shifted(): return lax.ppermute(block, axis, route)  33.6 us
    dot_general x7, matrix products, contract_rows(): lax.dot_general(left, right, (((0,), (0,)), ((), ())), preferred_element_...  23.3 us
  transfers between devices with their start and end apart: 18, of which 5 were waited for; matrix products, arithmetic and copies ran while one was open for 11% of the time, Pallas kernels for 0%

commit v1 on v0

--- a/solution.py
+++ b/solution.py
@@ -1,9 +1,16 @@
+import functools
 import math
 
 import jax
 import jax.numpy as jnp
+import numpy as np
 from jax import lax
+from jax.experimental import pallas as pl
+from jax.experimental.pallas import tpu as pltpu
 from jax.sharding import PartitionSpec as P
+
+MESH = pl.DeviceIdType.MESH
+LANES = 128
 
 D = 640
 HEADS = 4
@@ -88,6 +95,727 @@
 
 def flatten_all(arrays):
     return jnp.concatenate([array_item.reshape(-1) for array_item in arrays])
+
+
+class Place:
+    def __init__(self):
+        self.devices_seq = lax.axis_size("seq")
+        self.outer = self.devices_seq // 4
+        self.count = 2 * self.devices_seq
+        self.b = lax.axis_index("batch")
+        s = lax.axis_index("seq")
+        self.hi = lax.div(s, 4)
+        self.y = lax.rem(lax.div(s, 2), 2)
+        self.c = lax.rem(s, 2)
+
+    def block(self, b, hi, y, c):
+        return b * self.devices_seq + hi * 4 + y * 2 + c
+
+    def seq_id(self, hi, y, c):
+        return (self.b, hi * 4 + y * 2 + c)
+
+    def mine(self):
+        return self.block(self.b, self.hi, self.y, self.c)
+
+    def x_peer(self):
+        return (1 - self.b, self.hi * 4 + self.y * 2 + self.c)
+
+    def y_peer(self):
+        return self.seq_id(self.hi, 1 - self.y, self.c)
+
+    def sibling(self):
+        return self.seq_id(self.hi, self.y, 1 - self.c)
+
+    def outer_at(self, k):
+        return lax.rem(self.hi + k, self.outer)
+
+    def outer_peer(self, k):
+        return self.seq_id(self.outer_at(k), self.y, self.c)
+
+    def peers(self):
+        return [self.x_peer(), self.y_peer(), self.sibling()] + [
+            self.outer_peer(k) for k in range(1, self.outer)
+        ]
+
+
+def greet(place):
+    barrier = pltpu.get_barrier_semaphore()
+    peers = place.peers()
+    for peer in peers:
+        pl.semaphore_signal(barrier, inc=1, device_id=peer, device_id_type=MESH)
+    pl.semaphore_wait(barrier, len(peers))
+
+
+class Wires:
+    def __init__(self, send_sems, recv_sems):
+        self.send_sems, self.recv_sems = send_sems, recv_sems
+        self.used = 0
+        self.sent = []
+
+    def copy(self, src, dst, peer):
+        made = pltpu.make_async_remote_copy(
+            src_ref=src,
+            dst_ref=dst,
+            send_sem=self.send_sems.at[self.used],
+            recv_sem=self.recv_sems.at[self.used],
+            device_id=peer,
+            device_id_type=MESH,
+        )
+        self.used += 1
+        self.sent.append(made)
+        made.start()
+        return made
+
+    def drain(self):
+        for made in self.sent:
+            made.wait_send()
+        self.sent = []
+
+
+def gather_wires(outer):
+    return outer - 1 + 4 * outer + 4 * outer
+
+
+class Gather:
+    def __init__(self, place, wires, held, cut):
+        self.place, self.wires, self.held, self.cut = place, wires, held, cut
+        self.rows = held.shape[1]
+        self.from_outer = {}
+        self.from_x, self.from_y, self.diag, self.twin = {}, {}, {}, []
+
+    def part(self, index, first=0, last=None):
+        last = self.rows if last is None else last
+        if first == 0 and last == self.rows:
+            return self.held.at[index]
+        return self.held.at[index, pl.ds(first, last - first)]
+
+    def send(self, index, peer, first=0, last=None):
+        ref = self.part(index, first, last)
+        return self.wires.copy(ref, ref, peer)
+
+    def begin(self):
+        p = self.place
+        for k in range(1, p.outer):
+            self.from_outer[k] = self.send(p.mine(), p.outer_peer(k))
+        self.spread(0)
+
+    def spread(self, j):
+        p = self.place
+        if j:
+            self.from_outer[j].wait_recv()
+        index = p.block(p.b, p.outer_at(p.outer - j), p.y, p.c)
+        self.from_y[j] = self.send(index, p.y_peer())
+        self.from_x[j] = self.send(index, p.x_peer())
+        self.twin.append(self.send(index, p.sibling()))
+
+    def corner(self, j):
+        p = self.place
+        at = p.outer_at(p.outer - j)
+        self.from_y[j].wait_recv()
+        got = p.block(p.b, at, 1 - p.y, p.c)
+        down = self.send(got, p.x_peer(), 0, self.cut)
+        self.twin.append(self.send(got, p.sibling()))
+        self.from_x[j].wait_recv()
+        got = p.block(1 - p.b, at, p.y, p.c)
+        across = self.send(got, p.y_peer(), self.cut)
+        self.twin.append(self.send(got, p.sibling()))
+        self.diag[j] = (down, across)
+
+    def finish(self, j):
+        p = self.place
+        for made in self.diag[j]:
+            made.wait_recv()
+        self.twin.append(
+            self.send(p.block(1 - p.b, p.outer_at(p.outer - j), 1 - p.y, p.c), p.sibling())
+        )
+
+    def end(self):
+        for made in self.twin:
+            made.wait_recv()
+
+
+class Blocks:
+    def __init__(self, length, count):
+        self.length, self.count = length, count
+        self.stride, self.rest = divmod(length, LANES)
+        needed = -(-(length + self.rest * (count - 1)) // LANES)
+        self.rows = -(-needed // 16) * 16
+        self.tail = self.rows - self.stride
+        self.total = length * count
+
+    def pad(self, shard):
+        return jnp.pad(shard, (0, self.rows * LANES - self.length)).reshape(self.rows, LANES)
+
+    def take(self, block, index):
+        return lax.dynamic_slice(block.reshape(-1), (self.rest * index,), (self.length,))
+
+    def join(self, held):
+        first = held[:, : self.stride]
+        tails = jnp.concatenate([jnp.zeros_like(held[:1, self.stride :]), held[:-1, self.stride :]])
+        top = first[:, : self.tail] + tails
+        whole = jnp.concatenate([top, first[:, self.tail :]], axis=1).reshape(-1)
+        return jnp.concatenate([whole, held[-1, self.stride :].reshape(-1)])[: self.total]
+
+    def split(self, flat):
+        room = self.count * self.stride * LANES + self.tail * LANES
+        rows = jnp.pad(flat, (0, room - self.total)).reshape(-1, LANES)
+        first = rows[: self.count * self.stride].reshape(self.count, self.stride, LANES)
+        last = rows[self.count * self.stride :]
+        tails = jnp.concatenate([first[1:, : self.tail], last[None]])
+        return jnp.concatenate([first, tails], axis=1)
+
+
+class Scatter:
+    def __init__(self, place, wires, held, lands, result, first, last):
+        self.place, self.wires, self.held, self.result = place, wires, held, result
+        self.by_core, self.by_x, self.by_y, self.by_outer = lands
+        self.first, self.last = first, last
+        self.cut = first + (last - first) // 32 * 16
+
+    def rows(self, first, last):
+        return pl.ds(first, last - first)
+
+    def add(self, index, land, at, first, last):
+        rows = self.rows(first, last)
+        self.held[index, rows] = (
+            self.held[index, rows].astype(jnp.float32) + land[at, rows].astype(jnp.float32)
+        ).astype(self.held.dtype)
+
+    def core(self):
+        p, rows = self.place, self.rows(self.first, self.last)
+        self.from_core = []
+        for i in range(2 * p.outer * 2):
+            b, hi, y = i // (2 * p.outer), i // 2 % p.outer, i % 2
+            self.from_core.append(
+                self.wires.copy(
+                    self.held.at[p.block(b, hi, y, 1 - p.c), rows],
+                    self.by_core.at[i, rows],
+                    p.sibling(),
+                )
+            )
+
+    def plane(self):
+        p = self.place
+        for i, made in enumerate(self.from_core):
+            b, hi, y = i // (2 * p.outer), i // 2 % p.outer, i % 2
+            made.wait_recv()
+            self.add(p.block(b, hi, y, p.c), self.by_core, i, self.first, self.last)
+        self.from_x, self.from_y = [], []
+        for i in range(2 * p.outer):
+            hi, other = i // 2, i % 2
+            rows = self.rows(self.first, self.cut)
+            self.from_x.append(
+                self.wires.copy(
+                    self.held.at[p.block(1 - p.b, hi, other, p.c), rows],
+                    self.by_x.at[i, rows],
+                    p.x_peer(),
+                )
+            )
+            rows = self.rows(self.cut, self.last)
+            self.from_y.append(
+                self.wires.copy(
+                    self.held.at[p.block(other, hi, 1 - p.y, p.c), rows],
+                    self.by_y.at[i, rows],
+                    p.y_peer(),
+                )
+            )
+
+    def cross(self):
+        p = self.place
+        for i, (made_x, made_y) in enumerate(zip(self.from_x, self.from_y)):
+            hi, other = i // 2, i % 2
+            made_x.wait_recv()
+            self.add(p.block(p.b, hi, other, p.c), self.by_x, i, self.first, self.cut)
+            made_y.wait_recv()
+            self.add(p.block(other, hi, p.y, p.c), self.by_y, i, self.cut, self.last)
+        self.over_x, self.over_y = [], []
+        for hi in range(p.outer):
+            rows = self.rows(self.first, self.cut)
+            self.over_y.append(
+                self.wires.copy(
+                    self.held.at[p.block(p.b, hi, 1 - p.y, p.c), rows],
+                    self.by_y.at[hi, rows],
+                    p.y_peer(),
+                )
+            )
+            rows = self.rows(self.cut, self.last)
+            self.over_x.append(
+                self.wires.copy(
+                    self.held.at[p.block(1 - p.b, hi, p.y, p.c), rows],
+                    self.by_x.at[hi, rows],
+                    p.x_peer(),
+                )
+            )
+
+    def column(self):
+        p = self.place
+        for hi in range(p.outer):
+            index = p.block(p.b, hi, p.y, p.c)
+            self.over_y[hi].wait_recv()
+            self.add(index, self.by_y, hi, self.first, self.cut)
+            self.over_x[hi].wait_recv()
+            self.add(index, self.by_x, hi, self.cut, self.last)
+        rows = self.rows(self.first, self.last)
+        self.from_outer = []
+        for k in range(1, p.outer):
+            self.from_outer.append(
+                self.wires.copy(
+                    self.held.at[p.block(p.b, p.outer_at(k), p.y, p.c), rows],
+                    self.by_outer.at[k - 1, rows],
+                    p.outer_peer(k),
+                )
+            )
+
+    def end(self):
+        rows = self.rows(self.first, self.last)
+        total = self.held[self.place.mine(), rows].astype(jnp.float32)
+        for k, made in enumerate(self.from_outer):
+            made.wait_recv()
+            total = total + self.by_outer[k, rows].astype(jnp.float32)
+        self.result[rows] = total
+
+
+def scatter_wires(outer):
+    return 4 * outer + 4 * outer + 2 * outer + outer - 1
+
+
+def land_shapes(rows, outer):
+    return [
+        pltpu.VMEM((4 * outer, rows, LANES), jnp.bfloat16),
+        pltpu.VMEM((2 * outer, rows, LANES), jnp.bfloat16),
+        pltpu.VMEM((2 * outer, rows, LANES), jnp.bfloat16),
+        pltpu.VMEM((outer - 1, rows, LANES), jnp.bfloat16),
+    ]
+
+
+def scatter_kernel(pieces, attention_held, feed_held, attention_out, feed_out, *scratch):
+    lands_attention, lands_feed, (send, recv) = scratch[:4], scratch[4:8], scratch[8:]
+    place = Place()
+    greet(place)
+    wires = Wires(send, recv)
+    parts = []
+    for which, first, last in pieces:
+        held, lands, out = (
+            (attention_held, lands_attention, attention_out)
+            if which == 0
+            else (feed_held, lands_feed, feed_out)
+        )
+        parts.append(Scatter(place, wires, held, lands, out, first, last))
+    stages = [Scatter.core, Scatter.plane, Scatter.cross, Scatter.column, Scatter.end]
+    for step in range(len(parts) + len(stages) - 1):
+        for at in reversed(range(len(stages))):
+            if 0 <= step - at < len(parts):
+                stages[at](parts[step - at])
+    wires.drain()
+
+
+def scatter_all(attention_held, feed_held, outer):
+    rows = [attention_held.shape[1], feed_held.shape[1]]
+    middle = rows[1] // 32 * 16
+    pieces = [(1, 0, middle), (1, middle, rows[1]), (0, 0, rows[0])]
+    wires = len(pieces) * scatter_wires(outer)
+    return pl.pallas_call(
+        functools.partial(scatter_kernel, pieces),
+        out_shape=[jax.ShapeDtypeStruct((count, LANES), jnp.float32) for count in rows],
+        in_specs=[pl.BlockSpec(memory_space=pltpu.VMEM)] * 2,
+        out_specs=[pl.BlockSpec(memory_space=pltpu.VMEM)] * 2,
+        scratch_shapes=land_shapes(rows[0], outer)
+        + land_shapes(rows[1], outer)
+        + [pltpu.SemaphoreType.DMA((wires,)), pltpu.SemaphoreType.DMA((wires,))],
+        compiler_params=pltpu.CompilerParams(
+            collective_id=1, has_side_effects=True, vmem_limit_bytes=56 << 20
+        ),
+    )(attention_held, feed_held)
+
+
+EPS = 1e-06
+
+
+def root_inverse(rows):
+    return lax.rsqrt(jnp.mean(rows * rows, axis=-1, keepdims=True) + EPS)
+
+
+def turn(rows, cosine, sine):
+    half = rows.shape[-1] // 2
+    first, second = rows[:, :half], rows[:, half:]
+    return jnp.concatenate([first * cosine - second * sine, second * cosine + first * sine], axis=-1)
+
+
+def turn_back(rows, cosine, sine):
+    half = rows.shape[-1] // 2
+    first, second = rows[:, :half], rows[:, half:]
+    return jnp.concatenate([first * cosine + second * sine, second * cosine - first * sine], axis=-1)
+
+
+def dot_nn(left, right):
+    return jnp.dot(left, right, preferred_element_type=jnp.float32)
+
+
+def dot_nt(left, right):
+    return lax.dot_general(left, right, (((1,), (1,)), ((), ())), preferred_element_type=jnp.float32)
+
+
+def dot_tn(left, right):
+    return lax.dot_general(left, right, (((0,), (0,)), ((), ())), preferred_element_type=jnp.float32)
+
+
+def align_shard(blocks, place, padded_ref, shifted, aligned):
+    offset = blocks.rest * place.mine()
+    down, right = lax.div(offset, LANES), lax.rem(offset, LANES)
+    rows = blocks.rows
+    shifted[0:16] = jnp.zeros((16, LANES), jnp.float32)
+    shifted[16 : 16 + rows] = pltpu.roll(padded_ref[...].astype(jnp.float32), right, 1)
+    lane = lax.broadcasted_iota(jnp.int32, (rows, LANES), 1)
+    aligned[...] = jnp.where(
+        lane >= right, shifted[pl.ds(16 - down, rows)], shifted[pl.ds(15 - down, rows)]
+    ).astype(aligned.dtype)
+
+
+def flatten_held(blocks, held, flat):
+    stride, tail, rows = blocks.stride, blocks.tail, blocks.rows
+    if stride % 16 == 0 and tail == 16:
+        flat[0:tail] = held[0, 0:tail].astype(jnp.float32)
+        flat[tail:rows] = held[0, tail:rows].astype(jnp.float32)
+
+        def body(d, carry):
+            start = pl.multiple_of(d * stride, 16)
+            flat[pl.ds(start, tail)] += held[d, 0:tail].astype(jnp.float32)
+            start = pl.multiple_of(d * stride + tail, 16)
+            flat[pl.ds(start, stride)] = held[d, tail:rows].astype(jnp.float32)
+            return carry
+
+        lax.fori_loop(1, blocks.count, body, 0)
+    else:
+        flat[...] = jnp.zeros_like(flat)
+
+        def body(d, carry):
+            flat[pl.ds(d * stride, rows)] += held[d].astype(jnp.float32)
+            return carry
+
+        lax.fori_loop(0, blocks.count, body, 0)
+
+
+def unflatten(flat, base, matrix, first, width):
+    height, steps = matrix.shape[0], width // LANES
+    for i in range(steps):
+        matrix[:, first + i * LANES : first + (i + 1) * LANES] = flat[
+            pl.ds(base + i, height, stride=steps), :
+        ].astype(matrix.dtype)
+
+
+def read_gain(flat, base, width):
+    return jnp.concatenate([flat[base + i : base + i + 1, :] for i in range(width // LANES)], axis=-1)
+
+
+class Halo:
+    def __init__(self, place, wires, kv, block, first, size):
+        self.place, self.wires, self.kv, self.block = place, wires, kv, block
+        self.first, self.size = first, size
+
+    def slot(self, at):
+        return self.kv.at[pl.ds(self.first, self.size), pl.ds(pl.multiple_of(at * self.block, 128), self.block)]
+
+    def outward(self):
+        p = self.place
+        self.outer = self.wires.copy(self.slot(4), self.slot(0), p.outer_peer(1))
+
+    def plane(self):
+        p = self.place
+        self.outer.wait_recv()
+        self.across = self.wires.copy(self.slot(4 * (1 - p.y)), self.slot(2), p.y_peer())
+        self.near = self.wires.copy(self.slot(4 * (1 - p.c)), self.slot(3 - 2 * p.c), p.sibling())
+
+    def relay(self):
+        p = self.place
+        self.across.wait_recv()
+        self.far = self.wires.copy(self.slot(2), self.slot(1 + 2 * p.c), p.sibling())
+
+    def end(self):
+        self.near.wait_recv()
+        self.far.wait_recv()
+
+
+HALO_WIRES = 4
+
+
+class Locals:
+    def __init__(self, sems):
+        self.sems, self.used, self.open = sems, 0, []
+
+    def copy(self, src, dst):
+        made = pltpu.make_async_copy(src, dst, self.sems.at[self.used])
+        self.used += 1
+        self.open.append(made)
+        made.start()
+        return made
+
+    def finish(self, made):
+        made.wait()
+        self.open.remove(made)
+
+    def drain(self):
+        for made in self.open:
+            made.wait()
+        self.open = []
+
+
+class Geo:
+    def __init__(self, tokens, attention_params, feed_params):
+        self.seqs, self.block = tokens.shape[:2]
+        self.rows = self.seqs * self.block
+        self.count = lax.axis_size("batch") * lax.axis_size("seq")
+        self.outer = lax.axis_size("seq") // 4
+        self.attention = Blocks(attention_params.shape[0], self.count)
+        self.feed = Blocks(feed_params.shape[0], self.count)
+        self.reach = 5 * self.block
+
+
+QUERY = HEADS * HEAD_DIM
+BASE_KEY = D * QUERY // LANES
+BASE_VALUE = BASE_KEY + D * HEAD_DIM // LANES
+BASE_OUT = BASE_VALUE + D * HEAD_DIM // LANES
+BASE_GAINS = BASE_OUT + QUERY * D // LANES
+STEP = 256
+
+
+def forward_kernel(geo, tokens, positions, frequency, attention_in, feed_in, *refs):
+    (
+        feed_held,
+        out_wqkv,
+        out_wo,
+        out_gains,
+        out_q,
+        out_kv,
+        out_merged,
+        out_projected,
+        out_hidden,
+        out_cosine,
+        out_sine,
+    ) = refs[:11]
+    (
+        held,
+        own_feed,
+        shifted,
+        flat,
+        wqkv,
+        wo,
+        gains,
+        cosine,
+        sine,
+        lows,
+        normed,
+        q,
+        kv,
+        scores,
+        probs,
+        merged,
+        projected,
+        hidden,
+        send,
+        recv,
+        local,
+    ) = refs[11:]
+    place = Place()
+    wires, locals_ = Wires(send, recv), Locals(local)
+    seqs, block, reach = geo.seqs, geo.block, geo.reach
+    align_shard(geo.attention, place, attention_in, shifted, held.at[place.mine()])
+    align_shard(geo.feed, place, feed_in, shifted, own_feed)
+    lead = locals_.copy(own_feed, feed_held.at[place.mine()])
+    greet(place)
+    gather_a = Gather(place, wires, held, geo.attention.rows // 32 * 16)
+    gather_f = Gather(place, wires, feed_held, geo.feed.rows // 32 * 16)
+    gather_a.begin()
+
+    columns = positions[...].astype(jnp.float32).T
+    row = lax.broadcasted_iota(jnp.int32, (block, LANES), 0)
+    for s in range(seqs):
+        spot = columns[:, s : s + 1]
+        angle = spot * frequency[...]
+        rows = slice(s * block, (s + 1) * block)
+        cosine[rows] = jnp.cos(angle)
+        sine[rows] = jnp.sin(angle)
+        lows[s] = jnp.maximum(row + 1, row + WINDOW - spot.astype(jnp.int32))
+
+    gather_a.corner(0)
+    for j in range(1, geo.outer):
+        gather_a.spread(j)
+        gather_a.corner(j)
+        gather_a.finish(j - 1)
+    gather_a.finish(geo.outer - 1)
+    locals_.finish(lead)
+    gather_f.begin()
+    gather_a.end()
+    pending = [functools.partial(gather_f.corner, 0)]
+    for j in range(1, geo.outer):
+        pending.append(functools.partial(gather_f.spread, j))
+        pending.append(functools.partial(gather_f.corner, j))
+        pending.append(functools.partial(gather_f.finish, j - 1))
+    pending.append(functools.partial(gather_f.finish, geo.outer - 1))
+
+    def tick(amount=1):
+        for _ in range(amount):
+            if pending:
+                pending.pop(0)()
+
+    flatten_held(geo.attention, held, flat)
+    at = BASE_GAINS
+    for i, width in enumerate((D, HEAD_DIM, HEAD_DIM, D)):
+        gains[i : i + 1, :width] = read_gain(flat, at, width)
+        at += width // LANES
+    unflatten(flat, BASE_KEY, wqkv, QUERY, HEAD_DIM)
+    unflatten(flat, BASE_VALUE, wqkv, QUERY + HEAD_DIM, HEAD_DIM)
+    gain = gains[0:1, :]
+    gain_key = gains[2:3, :HEAD_DIM]
+    halos = []
+    per_step = STEP // block
+    for s in range(0, seqs, per_step):
+        rows = slice(s * block, (s + per_step) * block)
+        x = tokens[rows].astype(jnp.float32)
+        normed[rows] = (x * root_inverse(x) * gain).astype(jnp.bfloat16)
+        made = dot_nn(normed[rows], wqkv[:, QUERY:])
+        keys = made[:, :HEAD_DIM]
+        keys = turn(keys * root_inverse(keys) * gain_key, cosine[rows], sine[rows])
+        for i in range(per_step):
+            part = slice(i * block, (i + 1) * block)
+            kv[s + i, reach - block :, :HEAD_DIM] = keys[part].astype(jnp.bfloat16)
+            kv[s + i, reach - block :, HEAD_DIM:] = made[part, HEAD_DIM:].astype(jnp.bfloat16)
+        if (s + per_step) % (seqs // 2) == 0:
+            halo = Halo(place, wires, kv, block, s + per_step - seqs // 2, seqs // 2)
+            halo.outward()
+            halos.append(halo)
+    unflatten(flat, 0, wqkv, 0, QUERY)
+    tick(2)
+    gain_query = gains[1:2, :HEAD_DIM] * HEAD_DIM**-0.5
+    for s in range(0, seqs, per_step):
+        rows = slice(s * block, (s + per_step) * block)
+        made = dot_nn(normed[rows], wqkv[:, :QUERY])
+        for h in range(HEADS):
+            one = made[:, h * HEAD_DIM : (h + 1) * HEAD_DIM]
+            one = turn(one * root_inverse(one) * gain_query, cosine[rows], sine[rows])
+            q[h, rows] = one.astype(jnp.bfloat16)
+        tick()
+    unflatten(flat, BASE_OUT, wo, 0, D)
+    for src, dst in (
+        (wqkv, out_wqkv),
+        (wo, out_wo),
+        (gains, out_gains),
+        (q, out_q),
+        (cosine, out_cosine),
+        (sine, out_sine),
+    ):
+        locals_.copy(src, dst)
+    for halo in halos:
+        halo.plane()
+    tick()
+    for halo in halos:
+        halo.relay()
+    tick()
+
+    chunk = 32
+    lane = lax.broadcasted_iota(jnp.int32, (chunk, reach), 1)
+    over = lax.broadcasted_iota(jnp.int32, (chunk, reach), 1) - lax.broadcasted_iota(
+        jnp.int32, (chunk, reach), 0
+    )
+
+    def attend(s, carry):
+        start = pl.multiple_of(s * block, block)
+        rows = pl.ds(start, block)
+        queries = q[:, rows, :].reshape(HEADS * block, HEAD_DIM)
+        scores[...] = dot_nt(queries, kv[s, :, :HEAD_DIM])
+        for r in range(0, HEADS * block, chunk):
+            i = r % block
+            low = jnp.concatenate([lows[s, i : i + chunk, :]] * (reach // LANES), axis=-1)
+            seen = (lane >= low) & (over <= WINDOW + i)
+            raised = jnp.where(seen, jnp.exp(scores[r : r + chunk]), 0.0)
+            share = 1.0 / jnp.sum(raised, axis=-1, keepdims=True)
+            probs[r : r + chunk] = (raised * share).astype(jnp.bfloat16)
+        made = dot_nn(probs[...], kv[s, :, HEAD_DIM:])
+        for h in range(HEADS):
+            merged[rows, h * HEAD_DIM : (h + 1) * HEAD_DIM] = made[
+                h * block : (h + 1) * block
+            ].astype(jnp.bfloat16)
+        return carry
+
+    halves = seqs // 2
+    for g, halo in enumerate(halos):
+        halo.end()
+        for first in range(g * halves, (g + 1) * halves, 2):
+            lax.fori_loop(first, first + 2, attend, 0)
+            tick()
+    locals_.copy(kv, out_kv)
+    locals_.copy(merged, out_merged)
+    gain_post = gains[3:4, :]
+    for s in range(0, seqs, per_step):
+        rows = slice(s * block, (s + per_step) * block)
+        made = dot_nn(merged[rows], wo[...])
+        projected[rows] = made
+        hidden[rows] = tokens[rows].astype(jnp.float32) + made * root_inverse(made) * gain_post
+        locals_.copy(projected.at[rows], out_projected.at[rows])
+        locals_.copy(hidden.at[rows], out_hidden.at[rows])
+    tick(len(pending))
+    gather_f.end()
+    wires.drain()
+    locals_.drain()
+
+
+def vmem(shape, dtype):
+    return pltpu.VMEM(shape, dtype)
+
+
+def forward_pass(geo, tokens, positions, attention_block, feed_block):
+    count, rows, seqs, block = geo.count, geo.rows, geo.seqs, geo.block
+    bf, f4 = jnp.bfloat16, jnp.float32
+    half = HEAD_DIM // 2
+    frequency = (
+        rope_base ** (-(np.arange(half, dtype=np.float32) * np.float32(2.0) / HEAD_DIM))
+    ).astype(np.float32)[None]
+    wires = 2 * gather_wires(geo.outer) + 2 * HALO_WIRES
+    outs = [
+        ((count, geo.feed.rows, LANES), bf),
+        ((D, QUERY + 2 * HEAD_DIM), bf),
+        ((QUERY, D), bf),
+        ((8, D), f4),
+        ((HEADS, rows, HEAD_DIM), bf),
+        ((seqs, geo.reach, 2 * HEAD_DIM), bf),
+        ((rows, QUERY), bf),
+        ((rows, D), f4),
+        ((rows, D), f4),
+        ((rows, half), f4),
+        ((rows, half), f4),
+    ]
+    flat_rows = geo.attention.count * geo.attention.stride + geo.attention.tail
+    return pl.pallas_call(
+        functools.partial(forward_kernel, geo),
+        out_shape=[jax.ShapeDtypeStruct(*out) for out in outs],
+        in_specs=[pl.BlockSpec(memory_space=pltpu.VMEM)] * 5,
+        out_specs=[pl.BlockSpec(memory_space=pl.ANY)] * len(outs),
+        scratch_shapes=[
+            vmem((count, geo.attention.rows, LANES), bf),
+            vmem((geo.feed.rows, LANES), bf),
+            vmem((16 + geo.feed.rows, LANES), f4),
+            vmem((flat_rows, LANES), f4),
+            vmem((D, QUERY + 2 * HEAD_DIM), bf),
+            vmem((QUERY, D), bf),
+            vmem((8, D), f4),
+            vmem((rows, half), f4),
+            vmem((rows, half), f4),
+            vmem((seqs, block, LANES), jnp.int32),
+            vmem((rows, D), bf),
+            vmem((HEADS, rows, HEAD_DIM), bf),
+            vmem((seqs, geo.reach, 2 * HEAD_DIM), bf),
+            vmem((HEADS * block, geo.reach), f4),
+            vmem((HEADS * block, geo.reach), bf),
+            vmem((rows, QUERY), bf),
+            vmem((rows, D), f4),
+            vmem((rows, D), f4),
+            pltpu.SemaphoreType.DMA((wires,)),
+            pltpu.SemaphoreType.DMA((wires,)),
+            pltpu.SemaphoreType.DMA((32,)),
+        ],
+        compiler_params=pltpu.CompilerParams(
+            collective_id=0, has_side_effects=True, vmem_limit_bytes=60 << 20
+        ),
+    )(tokens.reshape(rows, D), positions, jnp.asarray(frequency), attention_block, feed_block)
 
 
 def on_device(tokens, attention_params, feed_params, positions, cotangent):
@@ -103,26 +831,18 @@
     for hop_index in range(hop_count, 0, -1):
         halo_starts[hop_index] = cursor
         cursor += needed_rows[hop_index - 1]
-    attention_flat, feed_flat = (
-        lax.all_gather(attention_params, ("batch", "seq"), axis=0, tiled=True),
-        lax.all_gather(feed_params, ("batch", "seq"), axis=0, tiled=True),
-    )
+    geo = Geo(tokens, attention_params, feed_params)
+    device = lax.axis_index("batch") * lax.axis_size("seq") + lax.axis_index("seq")
     (
-        weight_query,
-        weight_key,
-        weight_value,
-        weight_out,
-        gain_attention,
-        gain_query,
-        gain_key,
-        gain_post,
-    ) = split_flat(attention_flat, attention_layouts())
-    gain_attention = gain_attention.astype(jnp.float32)
-    gain_query = gain_query.astype(jnp.float32)
-    gain_key = gain_key.astype(jnp.float32)
-    gain_post = gain_post.astype(jnp.float32)
+        feed_held, wqkv, weight_out, gains, q, kv, merged, projected, hidden_state,
+        cosine_table, sine_table,
+    ) = forward_pass(
+        geo, tokens, positions, geo.attention.pad(attention_params), geo.feed.pad(feed_params)
+    )
+    feed_flat = geo.feed.join(feed_held)
+    weight_query, weight_key, weight_value = wqkv[:, :QUERY], wqkv[:, QUERY:QUERY+HEAD_DIM], wqkv[:, QUERY+HEAD_DIM:]
+    gain_attention, gain_query, gain_key, gain_post = gains[0], gains[1, :HEAD_DIM], gains[2, :HEAD_DIM], gains[3]
     inputs = tokens.astype(jnp.float32).reshape(total_rows, model_width)
-    cosine_table, sine_table = angles(positions.reshape(total_rows))
 
     def query_prep(raw_rows, scaling):
         return rotate(rms_norm(raw_rows, scaling), cosine_table[:, None, :], sine_table[:, None, :])
@@ -135,25 +855,8 @@
         total_rows, HEADS, HEAD_DIM
     )
     key_raw = jnp.dot(normed, weight_key, preferred_element_type=jnp.float32)
-    value_raw = jnp.dot(normed, weight_value, preferred_element_type=jnp.float32)
-    queries = (
-        query_prep(query_raw, gain_query)
-        .astype(jnp.bfloat16)
-        .reshape(seq_count, block, HEADS, HEAD_DIM)
-    )
-    key_rows = key_prep(key_raw, gain_key).astype(jnp.bfloat16).reshape(seq_count, block, HEAD_DIM)
-    value_rows = value_raw.astype(jnp.bfloat16).reshape(seq_count, block, HEAD_DIM)
-    halo_keys = []
-    halo_values = []
-    for hop_index in range(1, hop_count + 1):
-        needed = needed_rows[hop_index - 1]
-        got_keys, got_values = shifted(
-            (key_rows[:, block - needed :], value_rows[:, block - needed :]), "seq", hop_index
-        )
-        halo_keys.insert(0, got_keys)
-        halo_values.insert(0, got_values)
-    extended_keys = jnp.concatenate(halo_keys + [key_rows], axis=1)
-    extended_values = jnp.concatenate(halo_values + [value_rows], axis=1)
+    queries = (q.transpose(1, 0, 2) * 16).reshape(seq_count, block, HEADS, HEAD_DIM)
+    extended_keys, extended_values = kv[:, 1:, :HEAD_DIM], kv[:, 1:, HEAD_DIM:]
     extended_len = halo_rows + block
     distance = (
         jnp.arange(block, dtype=jnp.int32)[:, None]
@@ -171,19 +874,6 @@
         )
         return jnp.where(allowed, logits * score_scale, -1e30)
 
-    scores = score_of(queries, extended_keys)
-    row_peak = jnp.max(scores, axis=-1, keepdims=True)
-    raised = jnp.exp(scores - row_peak)
-    row_total = jnp.sum(raised, axis=-1, keepdims=True)
-    probability = raised / row_total
-    log_total = row_peak + jnp.log(row_total)
-    weights_rounded = probability.astype(jnp.bfloat16)
-    attended = jnp.einsum(
-        "shqk,skd->sqhd", weights_rounded, extended_values, preferred_element_type=jnp.float32
-    )
-    merged = attended.reshape(total_rows, HEADS * HEAD_DIM).astype(jnp.bfloat16)
-    projected = jnp.dot(merged, weight_out, preferred_element_type=jnp.float32)
-    hidden_state = inputs + rms_norm(projected, gain_post)
     weight_gate, weight_up, weight_down, gain_feed, gain_out = split_flat(feed_flat, feed_layouts())
     gain_feed = gain_feed.astype(jnp.float32)
     gain_out = gain_out.astype(jnp.float32)
@@ -227,7 +917,7 @@
         .reshape(seq_count, block, HEADS, HEAD_DIM)
     )
     scores = score_of(queries, extended_keys)
-    probability = jnp.exp(scores - log_total)
+    probability = jax.nn.softmax(scores, axis=-1)
     weights_rounded = probability.astype(jnp.bfloat16)
     grad_probs = jnp.einsum(
         "sqhd,skd->shqk", grad_merged, extended_values, preferred_element_type=jnp.float32
@@ -292,10 +982,13 @@
             grad_gain_post,
         ]
     )
-    attention_piece, feed_piece = (
-        lax.psum_scatter(attention_grads, ("batch", "seq"), scatter_dimension=0, tiled=True),
-        lax.psum_scatter(feed_grads, ("batch", "seq"), scatter_dimension=0, tiled=True),
-    )
+    attention_sum, feed_sum = scatter_all(
+        geo.attention.split(attention_grads).astype(jnp.bfloat16),
+        geo.feed.split(feed_grads).astype(jnp.bfloat16),
+        geo.outer,
+    )
+    attention_piece = geo.attention.take(attention_sum, device)
+    feed_piece = geo.feed.take(feed_sum, device)
     return (mixed, grad_tokens, attention_piece, feed_piece)
 
 

time: 1020 us -> 616 us (0.60); the launches traced: 1000 us -> 610 us
  waiting for transfers between devices: 608 us -> 19.8 us
  Pallas kernels: 0 us -> 181 us
  other arithmetic: 41.9 us -> 126 us
  local copies, waits for them, and re-layouts: 155 us -> 128 us
  starting transfers between devices: 33.7 us -> 10.6 us
  between operations: 15.3 us -> 1.69 us
    unnamed x4 -> x0, waiting for transfers between devices: 569 us -> none
    pallas_call x0 -> x2, Pallas kernels: none -> 181 us  [the longest x1 101 us: forward_pass(): pl.pallas_call(functools.partial(forward_kernel, geo), out_shape=[jax.Sha...]
    another operation x1 -> x2, other arithmetic: 4.12 us -> 61.9 us
    concatenate x2 -> x0, local copies, waits for them, and re-layouts: 25.8 us -> none  [the longest x1 20.2 us: on_device(): extended_keys = jnp.concatenate(halo_keys + [key_rows], axis=1)]
    ppermute x16 -> x8, starting transfers between devices: 33.6 us -> 10.6 us  [shifted(): return lax.ppermute(block, axis, route)]
    unnamed x174 -> x120, local copies, waits for them, and re-layouts: 59.8 us -> 37.8 us
    ppermute x16 -> x8, waiting for transfers between devices: 38.9 us -> 19.8 us  [shifted(): return lax.ppermute(block, axis, route)]
    sub x0 -> x1, other arithmetic: none -> 15.4 us  [on_device(): probability = jax.nn.softmax(scores, axis=-1)]
  transfers between devices with their start and end apart: 18 -> 8, of which waited for: 5 -> 2; matrix products, arithmetic and copies ran while one was open for 11% -> 29% of each run, Pallas kernels for 0% -> 0%
where the time goes in v1:
time: 616 us; the launch traced here: 610 us
  Pallas kernels  181 us (29%)
  matrix products  143 us (23%)
  local copies, waits for them, and re-layouts  128 us (21%)
  other arithmetic  126 us (20%)
  waiting for transfers between devices  19.8 us (3%)
  starting transfers between devices  10.6 us (2%)
    pallas_call x1, Pallas kernels, forward_pass(): pl.pallas_call(functools.partial(forward_kernel, geo), out_shape=[jax.Sha...  101 us
    pallas_call x1, Pallas kernels, scatter_all(): pl.pallas_call(functools.partial(scatter_kernel, pieces), out_shape=[jax....  79.1 us
    another operation x2, other arithmetic  61.9 us
    dot_general x7, matrix products, contract_cols(): lax.dot_general(left, right, (((1,), (1,)), ((), ())), preferred_element_...  39.8 us
    unnamed x120, local copies, waits for them, and re-layouts  37.8 us
    slice x2, local copies, waits for them, and re-layouts, split_flat(): pieces.append(flat_vector[offset:offset + length].reshape(layout))  26.8 us
    dot_general x7, matrix products, contract_rows(): lax.dot_general(left, right, (((0,), (0,)), ((), ())), preferred_element_...  20.4 us
    ppermute x8, waiting for transfers between devices, shifted(): return lax.ppermute(block, axis, route)  19.8 us
  transfers between devices with their start and end apart: 8, of which 2 were waited for; matrix products, arithmetic and copies ran while one was open for 29% of the time, Pallas kernels for 0%

profile of v1, /device:TPU:0, one launch (start us, length us, event | category | flops | bytes accessed | tf_op | source)
XLA Modules:
  0.0 609.8 jit_solution(16243916104857132575)
XLA Ops:
  3.8 101.5 %shard_map.123 = (bf16[32,976,128]{2,1,0:T(8,128)(2,1)}, bf16[640,1536]{1,0:T(8,128)(2,1)}, bf16[1024,640]{1,0:T(8,128)(2,1)}, f32[8,640]{1,0:T(8,128)}, bf16[4,...) custom-call(bf16[1024,640]{1,0:T(8,128)(2,1)} %bitcast.181, ...), custom_call_target="tpu_custom_call" | custom-call | tf_op jit(solution)/shard_map/pallas_call | solution.py:787
  106.9 3.7 slice.330
  111.6 4.0 pad_maximum_fusion
  115.6 12.7 %slice.331 = bf16[1920,2048]{1,0:T(8,128)(2,1)} reshape(bf16[32,960,128]{2,1,0:T(8,128)(2,1)} %pad_maximum_fusion) | data formatting | bytes 15728640 | tf_op jit(solution)/shard_map/slice | solution.py:61
  128.3 14.2 %slice.334 = bf16[6144,640]{1,0:T(8,128)(2,1)} reshape(bf16[32,960,128]{2,1,0:T(8,128)(2,1)} %pad_maximum_fusion) | data formatting | bytes 15728640 | tf_op jit(solution)/shard_map/slice | solution.py:61
  144.8 5.9 fusion.57
  150.7 7.7 %multiply_convert_fusion.1 = (bf16[1024,2048]{1,0:T(8,128)(2,1)}, f32[1024,2048]{1,0:T(8,128)}) fusion(f32[1024,2048]{1,0:T(8,128)S(1)} %fusion.57, bf16[1024,640]{1,0:T(8,128)(2,1)S(1)} %get-tuple-element.226, bf16[1920,2048]{1,0:T(8,128)(2,1)S(1)} %bitcast.199), kind=kOutput, calls=%fused_computation.20 | convolution fusion | flops 2705326080 | bytes 24903680 | tf_op jit(solution)/shard_map/dot_general | solution.py:886
  158.4 6.2 %multiply_reduce_fusion.8 = (f32[1024]{0:T(1024)S(1)}, f32[1024,640]{1,0:T(8,128)S(1)}) fusion(bf16[1024,2048]{1,0:T(8,128)(2,1)} %get-tuple-element.209, bf16[6144,640]{1,0:T(8,128)(2,1)} %slice.334), kind=kOutput, calls=%fused_computation.87 | convolution fusion | flops 2685664256 | bytes 9441280 | tf_op jit(solution)/shard_map/dot_general | solution.py:888
  167.9 14.8 %fusion.11 = (bf16[1024,2048]{1,0:T(8,128)(2,1)}, bf16[1024,2048]{1,0:T(8,128)(2,1)}) fusion(f32[1024,2048]{1,0:T(8,128)} %copy-done.42, f32[1024,2048]{1,0:T(8,128)} %get-tuple-element.210, bf16[1024,640]{1,0:T(8,128)(2,1)S(1)} %get-tuple-element.197, bf16[6144,640]{1,0:T(8,128)(2,1)} %slice.334), kind=kOutput, calls=%fused_computation.18 | convolution fusion | flops 2734686208 | bytes 29097984 | tf_op jit(solution)/shard_map/dot_general | solution.py:91
  182.8 5.9 fusion.51
  188.7 4.0 multiply_reduce_fusion.3
  193.5 2.5 multiply_reduce_fusion.4
  198.6 3.1 convolution_convert_fusion
  201.7 3.3 reshape.601
  207.0 7.3 %fusion.29 = f32[8,639,128,4]{2,1,3,0:T(8,128)} fusion(bf16[8,640,512]{2,1,0:T(8,128)(2,1)} %get-tuple-element.163, bf16[8,128,4,256]{3,2,1,0:T(4,128)(2,1)S(1)} %reshape.601), kind=kOutput, calls=%fused_computation.58 | convolution fusion | flops 1340080128 | bytes 15187968 | tf_op jit(solution)/shard_map/sqhd,skd->shqk/dot_general | solution.py:922
  214.3 5.0 fusion.40
  219.8 15.4 %fusion.104 = (f32[8,4,128]{2,1,0:T(4,128)S(1)}, f32[8,4,128,639]{2,3,1,0:T(8,128)}) fusion(f32[8,639,128,4]{2,1,3,0:T(8,128)} %fusion.40, pred[8,128,639]{1,2,0:T(8,128)(4,1)S(1)} %compare_and_fusion), kind=kOutput, calls=%fused_computation.194 | output fusion | flops 15704702 | bytes 21609472 | tf_op jit(solution)/shard_map/sub | solution.py:920
  235.2 19.0 %fusion.105 = (bf16[8,639,256]{2,1,0:T(8,128)(2,1)}, f32[8,639,256]{2,1,0:T(8,128)}) fusion(bf16[8,128,4,256]{3,1,0,2:T(8,128)(2,1)} %bitcast.197, f32[8,639,128,4]{2,1,3,0:T(8,128)} %fusion.29, f32[8,4,128,639]{2,3,1,0:T(8,128)} %get-tuple-element.215, f32[8,4,128]{2,1,0:T(4,128)S(1)} %get-tuple-element.214), kind=kOutput, calls=%fused_computation.195 | convolution fusion | flops 1359714944 | bytes 30904320 | tf_op jit(solution)/shard_map/shqk,sqhd->skd/dot_general | solution.py:930
  254.2 2.9 fusion.102
  264.2 8.8 %fusion.106 = (bf16[8,639,256]{2,1,0:T(8,128)(2,1)S(1)}, f32[8,639,256]{2,1,0:T(8,128)}) fusion(bf16[8,128,4,256]{3,2,1,0:T(4,128)(2,1)S(1)} %reshape.601, f32[8,4,128,639]{2,3,1,0:T(8,128)} %get-tuple-element.215, f32[8,4,128]{2,1,0:T(4,128)S(1)} %get-tuple-element.214), kind=kOutput, calls=%fused_computation.196 | convolution fusion | flops 1346623488 | bytes 20434944 | tf_op jit(solution)/shard_map/shqk,sqhd->skd/dot_general | solution.py:933
  276.0 5.1 fusion.108
  281.1 4.2 convolution_bitcast_fusion.1
  285.4 4.2 convolution_bitcast_fusion
  291.2 18.3 %fusion.61 = f32[8,128,4,256]{3,1,2,0:T(8,128)} fusion(f32[8,639,128,4]{2,1,3,0:T(8,128)} %fusion.29, bf16[8,640,512]{2,1,0:T(8,128)(2,1)} %get-tuple-element.163, f32[8,4,128,639]{2,3,1,0:T(8,128)} %get-tuple-element.215, f32[8,4,128]{2,1,0:T(4,128)S(1)} %get-tuple-element.214), kind=kOutput, calls=%fused_computation.109 | convolution fusion | flops 1358406272 | bytes 48791552 | tf_op jit(solution)/shard_map/shqk,skd->sqhd/dot_general | solution.py:927
  311.5 5.5 reshape.613
  317.0 2.7 copy.49
  322.2 43.3 %maximum_convert_fusion = bf16[3932160]{0:T(1024)(128)(2,1)S(1)} fusion(bf16[1310720]{0:T(1024)(128)(2,1)S(1)} %copy-done.6, bf16[1310720]{0:T(1024)(128)(2,1)S(1)} %bitcast.184, bf16[1310720]{0:T(1024)(128)(2,1)S(1)} %bitcast.187), kind=kLoop, calls=%fused_computation.2 | loop fusion | flops 23592960 | bytes 15728640 | tf_op jit(solution)/shard_map/convert.3
  365.6 3.1 copy-done.2
  369.5 3.0 copy-done.7
  381.7 2.5 copy.25
  388.5 2.9 copy.45
  396.9 2.5 copy.43
  399.4 3.7 multiply_reduce_fusion.2
  409.8 2.9 fusion.107
  412.8 2.8 reshape.609
  415.6 2.5 convert_dynamic-update-slice_fusion.4
  418.1 8.9 %maximum_maximum_fusion.feed_held = bf16[32,976,128]{2,1,0:T(8,128)(2,1)} fusion(bf16[1,16,128]{2,1,0:T(8,128)(2,1)S(1)} %copy-done.36, bf16[31,16,128]{2,1,0:T(8,128)(2,1)S(1)} %slice.380, bf16[32,960,128]{2,1,0:T(8,128)(2,1)} %bitcast.183), kind=kLoop, calls=%fused_computation.22 | loop fusion | flops 23986176 | bytes 15990784 | tf_op jit(solution)/shard_map/concatenate | solution.py:265
  427.0 5.3 fusion.71
  441.3 5.4 scatter-add.6
  450.4 3.1 fusion.79
  453.5 2.8 collective-permute-done.6
  458.3 16.9 %collective-permute-done.7 = bf16[8,127,256]{2,1,0:T(8,128)(2,1)} collective-permute-done((bf16[8,127,256]{2,1,0:T(8,128)(2,1)}, bf16[8,127,256]{2,1,0:T(8,128)(2,1)}, u32[]{:S(2)}, u32[]{:S(2)}) %collective-permute-start.7) | collective-permute-done | bytes 520224 | tf_op jit(solution)/shard_map/ppermute | solution.py:29
  477.4 5.4 scatter-add.9
  486.4 18.6 %maximum_convert_fusion.1 = bf16[1638400]{0:T(1024)(128)(2,1)S(1)} fusion(bf16[655360]{0:T(1024)(128)(2,1)S(1)} %reshape.609, bf16[163840]{0:T(1024)(128)(2,1)S(1)} %bitcast.202, bf16[163840]{0:T(1024)(128)(2,1)S(1)} %bitcast.200, bf16[655360]{0:T(1024)(128)(2,1)S(1)} %bitcast.192), kind=kLoop, calls=%fused_computation.26 | loop fusion | flops 13107200 | bytes 6553600 | tf_op jit(solution)/shard_map/convert.17
  508.6 3.6 fusion.34
  519.5 3.4 maximum_maximum_fusion.1.attention_held
  522.9 79.1 %shard_map.124 = (f32[416,128]{1,0:T(8,128)}, f32[976,128]{1,0:T(8,128)}) custom-call(bf16[32,416,128]{2,1,0:T(8,128)(2,1)} %maximum_maximum_fusion.1.attention_held, bf16[32,976,128]{2,1,0:T(8,128)(2,1)} %maximum_maximum_fusion.feed_held), custom_call_target="tpu_custom_call" | custom-call | tf_op jit(solution)/shard_map/pallas_call | solution.py:417
  605.8 3.9 fusion.27
  (195 shorter events, 94.7 us)
Async XLA Ops:
  128.3 14.3 %copy-start.1 = (f32[1024,640]{1,0:T(8,128)S(1)}, f32[1024,640]{1,0:T(8,128)}, u32[]{:S(2)}) copy-start(f32[1024,640]{1,0:T(8,128)} %get-tuple-element.161) | copy-start | bytes 7864324
  142.4 1.7 copy-start.5
  144.2 6.5 %slice-start.2 = ((s8[7864320]{0:T(1024)(128)(4,1)}), s8[4194304]{0:T(1024)(128)(4,1)S(1)}, s32[]{:S(2)}) async-start(s8[7864320]{0:T(1024)(128)(4,1)} %bitcast.198), calls=%async_computation.2 | async-start | bytes 8388608
  144.7 6.0 copy-start.33
  144.8 6.0 slice-start.3
  150.7 7.7 %copy-start.42 = (f32[1024,2048]{1,0:T(8,128)}, f32[1024,2048]{1,0:T(8,128)S(1)}, u32[]{:S(2)}) copy-start(f32[1024,2048]{1,0:T(8,128)S(1)} %fusion.57) | copy-start | bytes 25165828
  158.4 6.2 %copy-start.11 = (bf16[8,128,640]{2,1,0:T(8,128)(2,1)S(1)}, bf16[8,128,640]{2,1,0:T(8,128)(2,1)}, u32[]{:S(2)}) copy-start(bf16[8,128,640]{2,1,0:T(8,128)(2,1)} %param.38) | copy-start | bytes 3932164
  167.9 14.8 %copy-start.28 = (bf16[1024,640]{1,0:T(8,128)(2,1)}, bf16[1024,640]{1,0:T(8,128)(2,1)S(1)}, u32[]{:S(2)}) copy-start(bf16[1024,640]{1,0:T(8,128)(2,1)S(1)} %get-tuple-element.197) | copy-start | bytes 3932164
  182.7 5.9 copy-start.44
  196.0 2.6 copy-start.41
  205.1 9.2 %slice-start = ((s8[5242880]{0:T(1024)(128)(4,1)}), s8[4194304]{0:T(1024)(128)(4,1)S(1)}, s32[]{:S(2)}) async-start(s8[5242880]{0:T(1024)(128)(4,1)} %bitcast.193), calls=%async_computation | async-start | bytes 8388608
  207.0 7.3 %copy-start.17 = (bf16[4,1024,256]{2,1,0:T(8,128)(2,1)}, bf16[4,1024,256]{2,1,0:T(8,128)(2,1)S(1)}, u32[]{:S(2)}) copy-start(bf16[4,1024,256]{2,1,0:T(8,128)(2,1)S(1)} %broadcast_multiply_fusion) | copy-start | bytes 6291460
  207.0 7.3 %slice-start.1 = ((s8[5242880]{0:T(1024)(128)(4,1)}), s8[1048576]{0:T(1024)(128)(4,1)S(1)}, s32[]{:S(2)}) async-start(s8[5242880]{0:T(1024)(128)(4,1)} %bitcast.193), calls=%async_computation.1 | async-start | bytes 2097152
  214.3 5.0 copy-start.35
  257.1 175.1 %collective-permute-start = (bf16[8,128,256]{2,1,0:T(8,128)(2,1)}, bf16[8,128,256]{2,1,0:T(8,128)(2,1)}, u32[]{:S(2)}, u32[]{:S(2)}) collective-permute-start(bf16[8,128,256]{2,1,0:T(8,128)(2,1)} %get-tuple-element.202), channel_id=1, source_target_pairs={{1,0},{2,1},{3,2},{4,3},{5,4},{6,5},{7,6},{8,7},{9,8},{10,9},{11,1... | collective-permute-start | bytes 1572872 | tf_op jit(solution)/shard_map/ppermute | solution.py:29
  258.4 175.2 %collective-permute-start.1 = (bf16[8,128,256]{2,1,0:T(8,128)(2,1)}, bf16[8,128,256]{2,1,0:T(8,128)(2,1)}, u32[]{:S(2)}, u32[]{:S(2)}) collective-permute-start(bf16[8,128,256]{2,1,0:T(8,128)(2,1)} %get-tuple-element.204), channel_id=1, source_target_pairs={{2,0},{3,1},{4,2},{5,3},{6,4},{7,5},{8,6},{9,7},{10,8},{11,9},{12,... | collective-permute-start | bytes 1572872 | tf_op jit(solution)/shard_map/ppermute | solution.py:29
  259.7 175.2 %collective-permute-start.2 = (bf16[8,128,256]{2,1,0:T(8,128)(2,1)}, bf16[8,128,256]{2,1,0:T(8,128)(2,1)}, u32[]{:S(2)}, u32[]{:S(2)}) collective-permute-start(bf16[8,128,256]{2,1,0:T(8,128)(2,1)} %get-tuple-element.203), channel_id=1, source_target_pairs={{3,0},{4,1},{5,2},{6,3},{7,4},{8,5},{9,6},{10,7},{11,8},{12,9},{13... | collective-permute-start | bytes 1572872 | tf_op jit(solution)/shard_map/ppermute | solution.py:29
  262.9 175.3 %collective-permute-start.3 = (bf16[8,127,256]{2,1,0:T(8,128)(2,1)}, bf16[8,127,256]{2,1,0:T(8,128)(2,1)}, u32[]{:S(2)}, u32[]{:S(2)}) collective-permute-start(bf16[8,127,256]{2,1,0:T(8,128)(2,1)} %slice.372), channel_id=1, source_target_pairs={{4,0},{5,1},{6,2},{7,3},{8,4},{9,5},{10,6},{11,7},{12,8},{13,9},{1... | collective-permute-start | bytes 1560584 | tf_op jit(solution)/shard_map/ppermute | solution.py:29
  264.1 11.8 %copy-start.46 = (bf16[1024,2048]{1,0:T(8,128)(2,1)S(1)}, bf16[1024,2048]{1,0:T(8,128)(2,1)}, u32[]{:S(2)}) copy-start(bf16[1024,2048]{1,0:T(8,128)(2,1)} %get-tuple-element.209) | copy-start | bytes 12582916
  272.9 8.2 %copy-start.27 = (bf16[8,639,256]{2,1,0:T(8,128)(2,1)}, bf16[8,639,256]{2,1,0:T(8,128)(2,1)S(1)}, u32[]{:S(2)}) copy-start(bf16[8,639,256]{2,1,0:T(8,128)(2,1)S(1)} %get-tuple-element.222) | copy-start | bytes 7852036
  272.9 3.1 copy-start.29
  274.4 6.7 %copy-start.34 = (bf16[1024,640]{1,0:T(8,128)(2,1)S(1)}, bf16[1024,640]{1,0:T(8,128)(2,1)}, u32[]{:S(2)}) copy-start(bf16[1024,640]{1,0:T(8,128)(2,1)} %copy-done.33) | copy-start | bytes 3932164
  274.4 6.7 %copy-start.45 = (bf16[1024,2048]{1,0:T(8,128)(2,1)S(1)}, bf16[1024,2048]{1,0:T(8,128)(2,1)}, u32[]{:S(2)}) copy-start(bf16[1024,2048]{1,0:T(8,128)(2,1)} %get-tuple-element.189) | copy-start | bytes 12582916
  274.4 179.1 %collective-permute-start.4 = (bf16[8,128,256]{2,1,0:T(8,128)(2,1)}, bf16[8,128,256]{2,1,0:T(8,128)(2,1)}, u32[]{:S(2)}, u32[]{:S(2)}) collective-permute-start(bf16[8,128,256]{2,1,0:T(8,128)(2,1)} %get-tuple-element.199), channel_id=1, source_target_pairs={{1,0},{2,1},{3,2},{4,3},{5,4},{6,5},{7,6},{8,7},{9,8},{10,9},{11,1... | collective-permute-start | bytes 1572872 | tf_op jit(solution)/shard_map/ppermute | solution.py:29
  281.1 4.3 copy-start.43
  285.4 4.2 copy-start
  317.0 2.7 copy-start.21
  320.5 1.7 copy-start.6
  365.6 3.1 copy-start.2
  369.5 3.0 copy-start.7
  399.4 3.7 copy-start.16
  399.4 3.7 copy-start.23
  399.4 3.7 copy-start.24
  406.8 3.0 copy-start.40
  412.8 5.3 copy-start.36
  432.2 21.3 %collective-permute-start.5 = (bf16[8,128,256]{2,1,0:T(8,128)(2,1)}, bf16[8,128,256]{2,1,0:T(8,128)(2,1)}, u32[]{:S(2)}, u32[]{:S(2)}) collective-permute-start(bf16[8,128,256]{2,1,0:T(8,128)(2,1)} %get-tuple-element.201), channel_id=1, source_target_pairs={{2,0},{3,1},{4,2},{5,3},{6,4},{7,5},{8,6},{9,7},{10,8},{11,9},{12,... | collective-permute-start | bytes 1572872 | tf_op jit(solution)/shard_map/ppermute | solution.py:29
  433.5 22.8 %collective-permute-start.6 = (bf16[8,128,256]{2,1,0:T(8,128)(2,1)}, bf16[8,128,256]{2,1,0:T(8,128)(2,1)}, u32[]{:S(2)}, u32[]{:S(2)}) collective-permute-start(bf16[8,128,256]{2,1,0:T(8,128)(2,1)} %get-tuple-element.200), channel_id=1, source_target_pairs={{3,0},{4,1},{5,2},{6,3},{7,4},{8,5},{9,6},{10,7},{11,8},{12,9},{13... | collective-permute-start | bytes 1572872 | tf_op jit(solution)/shard_map/ppermute | solution.py:29
  434.9 40.4 %collective-permute-start.7 = (bf16[8,127,256]{2,1,0:T(8,128)(2,1)}, bf16[8,127,256]{2,1,0:T(8,128)(2,1)}, u32[]{:S(2)}, u32[]{:S(2)}) collective-permute-start(bf16[8,127,256]{2,1,0:T(8,128)(2,1)} %slice.378), channel_id=1, source_target_pairs={{4,0},{5,1},{6,2},{7,3},{8,4},{9,5},{10,6},{11,7},{12,8},{13,9},{1... | collective-permute-start | bytes 1560584 | tf_op jit(solution)/shard_map/ppermute | solution.py:29
  438.1 8.5 %copy-start.25 = (f32[1024,128]{1,0:T(8,128)S(1)}, f32[1024,128]{1,0:T(8,128)}, u32[]{:S(2)}) copy-start(f32[1024,128]{1,0:T(8,128)} %get-tuple-element.168) | copy-start | bytes 1572868
  441.3 7.0 %copy-start.37 = (f32[1,256]{1,0:T(1,128)S(1)}, f32[1,256]{1,0:T(1,128)}, u32[]{:S(2)}) copy-start(f32[1,256]{1,0:T(1,128)} %get-tuple-element.207) | copy-start | bytes 3076
  458.3 16.9 %copy-start.15 = (f32[8,128,256]{2,1,0:T(8,128)}, f32[8,128,256]{2,1,0:T(8,128)S(1)}, u32[]{:S(2)}) copy-start(f32[8,128,256]{2,1,0:T(8,128)S(1)} %fusion.75) | copy-start | bytes 3145732
  482.8 3.5 copy-start.10
  486.4 21.3 %copy-start.22 = (f32[1024,640]{1,0:T(8,128)S(1)}, f32[1024,640]{1,0:T(8,128)}, u32[]{:S(2)}) copy-start(f32[1024,640]{1,0:T(8,128)} %fusion.71) | copy-start | bytes 7864324
  505.0 7.3 %copy-start.8 = (bf16[1638400]{0:T(1024)(128)(2,1)}, bf16[1638400]{0:T(1024)(128)(2,1)S(1)}, u32[]{:S(2)}) copy-start(bf16[1638400]{0:T(1024)(128)(2,1)S(1)} %maximum_convert_fusion.1) | copy-start | bytes 9830404
  505.0 3.6 copy-start.12
  508.6 7.7 %copy-start.39 = (bf16[640]{0:T(1024)(128)(2,1)S(1)}, bf16[640]{0:T(1024)(128)(2,1)}, u32[]{:S(2)}) copy-start(bf16[640]{0:T(1024)(128)(2,1)} %get-tuple-element.178) | copy-start | bytes 3844
  517.5 1.9 copy-start.9
  522.9 82.9 %copy-start.4 = (f32[1024,640]{1,0:T(8,128)S(1)}, f32[1024,640]{1,0:T(8,128)}, u32[]{:S(2)}) copy-start(f32[1024,640]{1,0:T(8,128)} %copy-done.3) | copy-start | bytes 7864324
  (11 other events, 14.4 us)
